TPU v7x, 32 devices: a whole 2x2x4 slice. The times are simulated.
32 devices in a mesh: grp: 4 (over y, x), dev: 8 (over z, core).
Axes of the slice: x: 2, y: 2, z: 4, core: 2. Of those that a mesh axis runs over, the one named last changes fastest.
Arguments:
- boundary_heat_flux: float32 [4096, 4096], P('grp', 'dev'), may hold values from -6 to 6
- layer_kernel: float32 [2, 2, 2048, 4096], P(None, None, ('grp', 'dev')), may hold values from -6 to 6
Outputs:
- thermal_rise: float32 [2, 4096, 4096], P(None, 'grp', 'dev')
All inputs are finite; a program needn't handle non-finite values.
Results may differ from a plain program's by a relative error of at most 0.0001.
Values sent between devices are 32-bit elements; how exact they have to be, the bound alone decides.
A program may use at most 128 MiB of HBM per device.

v0:
```python
import math

import jax
import jax.numpy as jnp
from jax import lax
from jax.sharding import PartitionSpec as P


def split_length(length):
    leading = 1
    for candidate in range(1, math.isqrt(length) + 1):
        if length % candidate == 0 and candidate % 2 == 0:
            leading = candidate
    return (leading, length // leading)


def tables(leading, trailing, direction):
    length = leading * trailing
    outer_idx = lax.iota(jnp.int32, leading)
    inner_idx = lax.iota(jnp.int32, trailing)
    angle_outer = (outer_idx[:, None] * outer_idx[None, :] % leading).astype(jnp.float32) * (
        2.0 * math.pi / leading
    )
    angle_twist = (outer_idx[:, None] * inner_idx[None, :] % length).astype(jnp.float32) * (
        2.0 * math.pi / length
    )
    angle_inner = (inner_idx[:, None] * inner_idx[None, :] % trailing).astype(jnp.float32) * (
        2.0 * math.pi / trailing
    )
    return (
        jnp.cos(angle_outer),
        direction * jnp.sin(angle_outer),
        jnp.cos(angle_twist),
        direction * jnp.sin(angle_twist),
        jnp.cos(angle_inner),
        direction * jnp.sin(angle_inner),
    )


def contract(pattern, table, values):
    return jnp.einsum(
        pattern, table, values, precision=lax.Precision.HIGHEST, preferred_element_type=jnp.float32
    )


def section_outer(real_in, imag_in, table, pattern):
    cos_outer, sin_outer, cos_twist, sin_twist = (table[0], table[1], table[2], table[3])
    if imag_in is None:
        real_mid = contract(pattern, cos_outer, real_in)
        imag_mid = contract(pattern, sin_outer, real_in)
    else:
        real_mid = contract(pattern, cos_outer, real_in) - contract(pattern, sin_outer, imag_in)
        imag_mid = contract(pattern, cos_outer, imag_in) + contract(pattern, sin_outer, real_in)
    return (
        real_mid * cos_twist - imag_mid * sin_twist,
        imag_mid * cos_twist + real_mid * sin_twist,
    )


def section_inner(real_mid, imag_mid, table, pattern, real_only):
    cos_inner, sin_inner = (table[4], table[5])
    real_out = contract(pattern, cos_inner, real_mid) - contract(pattern, sin_inner, imag_mid)
    if real_only:
        return real_out
    imag_out = contract(pattern, cos_inner, imag_mid) + contract(pattern, sin_inner, real_mid)
    return (real_out, imag_out)


def reflect_first(values):
    return jnp.roll(jnp.flip(values, -1), 1, -1)


def into_frequency(real_part, imag_part):
    return (
        lax.all_to_all(
            lax.all_to_all(real_part, "grp", split_axis=0, concat_axis=3, tiled=True),
            "dev",
            split_axis=1,
            concat_axis=4,
            tiled=True,
        ),
        lax.all_to_all(
            lax.all_to_all(imag_part, "grp", split_axis=0, concat_axis=3, tiled=True),
            "dev",
            split_axis=1,
            concat_axis=4,
            tiled=True,
        ),
    )


def to_spatial(real_part, imag_part):
    return (
        lax.all_to_all(
            lax.all_to_all(real_part, "grp", split_axis=4, concat_axis=1, tiled=True),
            "dev",
            split_axis=5,
            concat_axis=2,
            tiled=True,
        ),
        lax.all_to_all(
            lax.all_to_all(imag_part, "grp", split_axis=4, concat_axis=1, tiled=True),
            "dev",
            split_axis=5,
            concat_axis=2,
            tiled=True,
        ),
    )


def body(boundary_heat_flux, layer_kernel):
    groups = lax.axis_size("grp")
    members = lax.axis_size("dev")
    columns = lax.all_to_all(boundary_heat_flux, "dev", split_axis=0, concat_axis=1, tiled=True)
    x_rows = columns.shape[0]
    width_y = columns.shape[1]
    width_x = groups * members * x_rows
    half_y = width_y // 2
    block_rows = half_y // (groups * members)
    lead_y, trail_y = split_length(width_y)
    leading_horizontal, trail_x = split_length(width_x)
    ahead_vertical = tables(lead_y, trail_y, -1.0)
    forward_x = tables(leading_horizontal, trail_x, -1.0)
    backward_x = tables(leading_horizontal, trail_x, 1.0)
    backward_y = tables(lead_y, trail_y, 1.0)
    device_pos = lax.axis_index("grp") * members + lax.axis_index("dev")
    first_row = jnp.logical_and(device_pos == 0, lax.iota(jnp.int32, block_rows) == 0)
    first_row = first_row.astype(jnp.float32)[:, None]
    real_mid, imag_mid = section_outer(
        columns.reshape(x_rows, lead_y, trail_y), None, ahead_vertical, "ap,rpq->raq"
    )
    real_spec, imag_spec = section_inner(real_mid, imag_mid, ahead_vertical, "bq,raq->bar", False)
    real_spec = real_spec.reshape(width_y, x_rows)
    imag_spec = imag_spec.reshape(width_y, x_rows)
    lower_shape = (groups, members, block_rows, x_rows)
    sides = 2
    real_remainder = jnp.roll(jnp.flip(real_spec, 0), 1, 0)[:half_y]
    imag_tail = jnp.roll(jnp.flip(imag_spec, 0), 1, 0)[:half_y]
    real_send = jnp.stack(
        [real_spec[:half_y].reshape(lower_shape), real_remainder.reshape(lower_shape)], axis=2
    )
    imag_send = jnp.stack(
        [imag_spec[:half_y].reshape(lower_shape), imag_tail.reshape(lower_shape)], axis=2
    )
    local_rows = sides * block_rows
    shape_sent = (groups, members, local_rows, 1, 1, x_rows)
    real_recv, imag_recv = into_frequency(
        real_send.reshape(shape_sent), imag_send.reshape(shape_sent)
    )
    real_mid, imag_mid = section_outer(
        real_recv.reshape(local_rows, leading_horizontal, trail_x),
        imag_recv.reshape(local_rows, leading_horizontal, trail_x),
        forward_x,
        "ap,rpq->raq",
    )
    real_freq, imag_freq = section_inner(real_mid, imag_mid, forward_x, "bq,raq->rba", False)
    real_freq = real_freq.reshape(local_rows, width_x)
    imag_freq = imag_freq.reshape(local_rows, width_x)
    norm_factor = 1.0 / (width_x * width_y)

    def inverse_x(kernel_pair):
        kernel_real = kernel_pair[0]
        kernel_imag = kernel_pair[1]
        keep_rows = 1.0 - first_row
        kernel_real = jnp.concatenate([kernel_real, reflect_first(kernel_real) * keep_rows], axis=0)
        kernel_imag = jnp.concatenate(
            [kernel_imag, -reflect_first(kernel_imag) * keep_rows], axis=0
        )
        real_prod = real_freq * kernel_real - imag_freq * kernel_imag
        imag_prod = real_freq * kernel_imag + imag_freq * kernel_real
        central_couple = section_outer(
            real_prod.reshape(local_rows, leading_horizontal, trail_x),
            imag_prod.reshape(local_rows, leading_horizontal, trail_x),
            backward_x,
            "ap,rpq->raq",
        )
        real_out, imag_out = section_inner(
            central_couple[0], central_couple[1], backward_x, "bq,raq->rba", False
        )
        real_out = real_out.reshape(local_rows, width_x)
        imag_out = imag_out.reshape(local_rows, width_x)
        shape_back = (1, 1, local_rows, groups, members, x_rows)
        return (real_out.reshape(shape_back), imag_out.reshape(shape_back))

    def inverse_y(real_part, imag_part):
        zero_row = jnp.zeros((1, x_rows), jnp.float32)

        def arrange(values):
            paired = values.reshape(groups * members, 2, block_rows, x_rows)
            lower = paired[:, 0].reshape(half_y, x_rows)
            upper = paired[:, 1].reshape(half_y, x_rows)
            return jnp.concatenate([lower, zero_row, jnp.flip(upper[1:], 0)], axis=0)

        central_couple = section_outer(
            arrange(real_part).reshape(lead_y, trail_y, x_rows),
            arrange(imag_part).reshape(lead_y, trail_y, x_rows),
            backward_y,
            "ap,pqr->raq",
        )
        real_out = section_inner(
            central_couple[0], central_couple[1], backward_y, "bq,raq->rba", True
        )
        return real_out.reshape(x_rows, width_y) * norm_factor

    def finish(kernels):
        real_back, imag_back = jax.vmap(inverse_x)(kernels)
        real_part, imag_part = to_spatial(real_back, imag_back)
        rows_done = jax.vmap(inverse_y)(real_part, imag_part)
        return lax.all_to_all(rows_done, "dev", split_axis=2, concat_axis=1, tiled=True)

    thermal_rise = jnp.concatenate(
        [
            finish(layer_kernel[layer_pos : layer_pos + 1])
            for layer_pos in range(layer_kernel.shape[0])
        ],
        axis=0,
    )
    return thermal_rise


def solution(mesh):
    placed = (P("grp", "dev"), P(None, None, ("grp", "dev"), None))
    return jax.shard_map(
        body, mesh=mesh, in_specs=placed, out_specs=P(None, "grp", "dev"), check_vma=False
    )
```

profile of v0, /device:TPU:0, one launch (start us, length us, event | category | flops | bytes accessed | tf_op | source)
XLA Modules:
  0.0 865.1 jit_solution(1786661798837099126)
XLA Ops:
  0.0 6.3 all-to-all-start
  6.8 48.6 %all-to-all-done = f32[8,128,512]{2,1,0:T(8,128)S(1)} async-done(((f32[8,128,512]{2,1,0:T(8,128)}), f32[8,128,512]{2,1,0:T(8,128)S(1)}, u32[]{:S(2)}, u32[]{:S(2)}) %all-to-all-start) | async-done | bytes 2097184 | tf_op jit(solution)/shard_map/all_to_all | solution.py:114
  63.1 5.8 subtract_bitcast_fusion.3
  78.4 17.1 %slice.140 = f32[4095,128]{1,0:T(8,128)} reverse(f32[4095,128]{1,0:T(8,128)} %slice.175), dimensions={0} | reverse | bytes 4193280 | tf_op jit(solution)/shard_map/jit(_roll_static)/slice | solution.py:138
  98.9 4.7 all-to-all-start.3
  103.6 4.8 fusion.80
  114.7 17.2 %slice.135 = f32[4095,128]{1,0:T(8,128)} reverse(f32[4095,128]{1,0:T(8,128)} %slice.172), dimensions={0} | reverse | bytes 4193280 | tf_op jit(solution)/shard_map/jit(_roll_static)/slice | solution.py:137
  135.3 4.2 all-to-all-start.1
  142.6 21.3 %all-to-all-done.1 = f32[4,8,128,1,1,128]{5,2,1,4,3,0:T(8,128)S(1)} async-done(((f32[4,8,128,1,1,128]{5,2,1,4,3,0:T(8,128)}), f32[4,8,128,1,1,128]{5,2,1,4,3,0:T(8,128)S(1)}, u32[]{:S(2)}, u32[]{:S(2)}) %all-to-all-start.1) | async-done | bytes 2097184 | tf_op jit(solution)/shard_map/all_to_all | solution.py:76
  165.2 3.6 all-to-all-start.4
  168.8 5.0 fusion.423
  176.2 16.2 %reverse.15 = f32[1,64,4096]{2,1,0:T(8,128)} reverse(f32[1,64,4096]{2,1,0:T(8,128)} %bitcast.474), dimensions={2} | reverse | bytes 2097152
  195.0 16.2 %reverse.14 = f32[1,64,4096]{2,1,0:T(8,128)} reverse(f32[1,64,4096]{2,1,0:T(8,128)} %bitcast.475), dimensions={2} | reverse | bytes 2097152
  212.5 16.2 %reverse.13 = f32[1,64,4096]{2,1,0:T(8,128)} reverse(f32[1,64,4096]{2,1,0:T(8,128)} %bitcast.476), dimensions={2} | reverse | bytes 2097152
  238.0 5.5 all-to-all-start.2
  254.9 4.2 copy.211
  265.1 4.3 copy.237
  269.4 11.3 %reverse.12 = f32[1,64,4096]{2,1,0:T(8,128)} reverse(f32[1,64,4096]{2,1,0:T(8,128)S(1)} %bitcast.470), dimensions={2} | reverse | bytes 2097152
  284.8 4.3 copy.240
  291.4 4.3 copy.207
  297.9 4.4 copy.212
  304.5 4.3 copy.238
  310.9 4.2 copy.241
  315.4 6.9 broadcast_multiply_fusion.3
  324.2 4.6 fusion.72
  328.9 4.7 fusion.70
  335.7 5.1 fusion.94
  340.9 4.5 fusion.20
  348.8 5.1 fusion.62
  357.3 10.1 %fusion.17 = (f32[128,64,64]{0,1,2:T(8,128)S(1)}, f32[128,64,64]{0,1,2:T(8,128)S(1)}, f32[128,64,64]{0,1,2:T(8,128)}, f32[128,64,64]{0,1,2:T(8,128)}) fusion(f32[128,64,64]{0,2,1:T(8,128)S(1)} %fusion.100, f32[64,64,64]{0,1,2:T(8,128)S(1)} %copy-done.23, f32[64,64,64]{0,1,2:T(8,128)S(1)} %copy-done.27, f32[64,64,64]{0,1,2:T(8,128)S(1)} %copy-done.22, ...), kind=kOutput, calls=%fused_computation.44 | convolution fusion | flops 411627520 | bytes 23068672 | tf_op jit(solution)/shard_map/bq,raq->rba/dot_general | solution.py:41
  377.2 3.6 fusion.54
  386.7 4.4 all-to-all-start.7
  391.1 4.8 fusion.56
  401.9 15.1 %all-to-all-done.7 = f32[1,1,1,128,4,8,128]{3,6,5,2,1,0,4:T(8,128)} async-done(((f32[1,1,1,128,4,8,128]{3,6,5,2,1,0,4:T(8,128)}), f32[1,1,1,128,4,8,128]{3,6,5,2,1,0,4:T(8,128)}, u32[]{:S(2)}, u32[]{:S(2)}) %all-to-all-start.7) | async-done | bytes 2097184 | tf_op jit(solution)/shard_map/all_to_all | solution.py:102
  417.0 3.6 all-to-all-start.5
  423.8 21.8 %all-to-all-done.5 = f32[1,1,1,128,4,8,128]{3,6,5,2,1,0,4:T(8,128)S(1)} async-done(((f32[1,1,1,128,4,8,128]{3,6,5,2,1,0,4:T(8,128)}), f32[1,1,1,128,4,8,128]{3,6,5,2,1,0,4:T(8,128)S(1)}, u32[]{:S(2)}, u32[]{:S(2)}) %all-to-all-start.5) | async-done | bytes 2097184 | tf_op jit(solution)/shard_map/all_to_all | solution.py:95
  445.6 4.3 all-to-all-start.8
  451.5 47.6 %all-to-all-done.8 = f32[1,4,1,128,1,8,128]{3,6,1,4,2,0,5:T(8,128)} async-done(((f32[1,4,1,128,1,8,128]{3,6,1,4,2,0,5:T(8,128)}), f32[1,4,1,128,1,8,128]{3,6,1,4,2,0,5:T(8,128)}, u32[]{:S(2)}, u32[]{:S(2)}) %all-to-all-start.8) | async-done | bytes 2097184 | tf_op jit(solution)/shard_map/all_to_all | solution.py:101
  499.1 4.8 all-to-all-start.6
  509.5 3.6 convolution_add_fusion
  517.2 3.6 concatenate.145
  520.8 4.8 fusion.46
  525.6 4.6 fusion.48
  530.2 22.7 %all-to-all-done.6 = f32[1,4,1,128,1,8,128]{3,6,1,4,2,0,5:T(8,128)} async-done(((f32[1,4,1,128,1,8,128]{3,6,1,4,2,0,5:T(8,128)}), f32[1,4,1,128,1,8,128]{3,6,1,4,2,0,5:T(8,128)}, u32[]{:S(2)}, u32[]{:S(2)}) %all-to-all-start.6) | async-done | bytes 2097184 | tf_op jit(solution)/shard_map/all_to_all | solution.py:94
  557.2 3.6 concatenate.144
  560.8 5.1 fusion.113
  569.4 6.1 fusion.9
  584.8 4.9 all-to-all-start.10
  589.8 4.8 fusion.38
  600.5 14.2 %all-to-all-done.10 = f32[1,1,1,128,4,8,128]{3,6,5,2,1,0,4:T(8,128)} async-done(((f32[1,1,1,128,4,8,128]{3,6,5,2,1,0,4:T(8,128)}), f32[1,1,1,128,4,8,128]{3,6,5,2,1,0,4:T(8,128)}, u32[]{:S(2)}, u32[]{:S(2)}) %all-to-all-start.10) | async-done | bytes 2097184 | tf_op jit(solution)/shard_map/all_to_all | solution.py:95
  614.8 3.6 all-to-all-start.12
  621.6 21.1 %all-to-all-done.12 = f32[1,1,1,128,4,8,128]{3,6,5,2,1,0,4:T(8,128)S(1)} async-done(((f32[1,1,1,128,4,8,128]{3,6,5,2,1,0,4:T(8,128)}), f32[1,1,1,128,4,8,128]{3,6,5,2,1,0,4:T(8,128)S(1)}, u32[]{:S(2)}, u32[]{:S(2)}) %all-to-all-start.12) | async-done | bytes 2097184 | tf_op jit(solution)/shard_map/all_to_all | solution.py:102
  642.7 4.4 all-to-all-start.11
  648.6 47.6 %all-to-all-done.11 = f32[1,4,1,128,1,8,128]{3,6,1,4,2,0,5:T(8,128)} async-done(((f32[1,4,1,128,1,8,128]{3,6,1,4,2,0,5:T(8,128)}), f32[1,4,1,128,1,8,128]{3,6,1,4,2,0,5:T(8,128)}, u32[]{:S(2)}, u32[]{:S(2)}) %all-to-all-start.11) | async-done | bytes 2097184 | tf_op jit(solution)/shard_map/all_to_all | solution.py:94
  696.2 4.5 all-to-all-start.13
  710.1 39.6 %all-to-all-done.13 = f32[1,4,1,128,1,8,128]{3,6,1,4,2,0,5:T(8,128)} async-done(((f32[1,4,1,128,1,8,128]{3,6,1,4,2,0,5:T(8,128)}), f32[1,4,1,128,1,8,128]{3,6,1,4,2,0,5:T(8,128)}, u32[]{:S(2)}, u32[]{:S(2)}) %all-to-all-start.13) | async-done | bytes 2097184 | tf_op jit(solution)/shard_map/all_to_all | solution.py:101
  749.8 4.4 all-to-all-start.9
  761.6 5.3 rev.24
  770.2 8.1 concatenate.158
  778.3 5.0 fusion.32
  790.0 4.8 fusion.1
  804.2 5.0 all-to-all-start.14
  812.1 46.1 %all-to-all-done.14 = f32[1,128,4096]{1,0,2:T(1,128)S(1)} async-done(((f32[1,128,4096]{1,0,2:T(1,128)}), f32[1,128,4096]{1,0,2:T(1,128)S(1)}, u32[]{:S(2)}, u32[]{:S(2)}) %all-to-all-start.14) | async-done | bytes 2097184 | tf_op jit(solution)/shard_map/all_to_all | solution.py:209
  860.0 4.7 pad_maximum_fusion
  (184 shorter events, 196.5 us)
Async XLA Ops:
  0.0 55.4 %all-to-all-start = ((f32[8,128,512]{2,1,0:T(8,128)}), f32[8,128,512]{2,1,0:T(8,128)S(1)}, u32[]{:S(2)}, u32[]{:S(2)}) async-start(f32[8,128,512]{2,1,0:T(8,128)} %bitcast.483), calls=%async_computation | async-start | bytes 4194304 | tf_op jit(solution)/shard_map/all_to_all | solution.py:114
  55.4 1.3 copy-start.19
  58.6 1.3 copy-start.4
  68.9 3.3 copy-start.3
  95.5 1.6 copy-start.21
  98.9 36.4 %all-to-all-start.3 = ((f32[4,8,128,1,1,128]{5,2,1,4,3,0:T(8,128)}), f32[4,8,128,1,1,128]{5,2,1,4,3,0:T(8,128)}, u32[]{:S(2)}, u32[]{:S(2)}) async-start(f32[4,8,128,1,1,128]{5,2,1,4,3,0:T(8,128)} %bitcast.449), calls=%async_computation.3 | async-start | bytes 4194304 | tf_op jit(solution)/shard_map/all_to_all | solution.py:83
  111.8 1.4 copy-start.8
  114.7 17.2 %copy-start.9 = (f32[64,64,128]{2,0,1:T(8,128)S(1)}, f32[64,64,128]{2,0,1:T(8,128)}, u32[]{:S(2)}) copy-start(f32[64,64,128]{2,0,1:T(8,128)} %copy-done.8) | copy-start | bytes 6291460
  131.9 1.6 copy-start.20
  135.3 28.6 %all-to-all-start.1 = ((f32[4,8,128,1,1,128]{5,2,1,4,3,0:T(8,128)}), f32[4,8,128,1,1,128]{5,2,1,4,3,0:T(8,128)S(1)}, u32[]{:S(2)}, u32[]{:S(2)}) async-start(f32[4,8,128,1,1,128]{5,2,1,4,3,0:T(8,128)} %bitcast.453), calls=%async_computation.1 | async-start | bytes 4194304 | tf_op jit(solution)/shard_map/all_to_all | solution.py:76
  163.9 1.3 copy-start.17
  165.2 71.5 %all-to-all-start.4 = ((f32[1,8,128,4,1,128]{5,2,3,4,0,1:T(8,128)}), f32[1,8,128,4,1,128]{5,2,3,4,0,1:T(8,128)S(1)}, u32[]{:S(2)}, u32[]{:S(2)}) async-start(f32[1,8,128,4,1,128]{5,2,3,4,0,1:T(8,128)} %copy.196), calls=%async_computation.4 | async-start | bytes 4194304 | tf_op jit(solution)/shard_map/all_to_all | solution.py:82
  173.9 1.0 copy-start.28
  229.5 3.0 copy-start.35
  231.2 2.7 copy-start.36
  232.6 2.7 copy-start.18
  236.7 1.3 copy-start.16
  238.0 95.5 %all-to-all-start.2 = ((f32[1,8,128,4,1,128]{5,2,3,4,0,1:T(8,128)}), f32[1,8,128,4,1,128]{5,2,3,4,0,1:T(8,128)}, u32[]{:S(2)}, u32[]{:S(2)}) async-start(f32[1,8,128,4,1,128]{5,2,3,4,0,1:T(8,128)} %copy.187), calls=%async_computation.2 | async-start | bytes 4194304 | tf_op jit(solution)/shard_map/all_to_all | solution.py:75
  243.5 2.7 copy-start.33
  259.1 3.5 copy-start.34
  265.1 4.3 copy-start.37
  284.8 4.3 copy-start.32
  291.4 4.3 copy-start.31
  297.9 4.4 copy-start.30
  304.5 4.3 copy-start.29
  335.7 5.1 copy-start.15
  345.4 11.8 %copy-start.27 = (f32[64,64,64]{0,1,2:T(8,128)S(1)}, f32[64,64,64]{0,1,2:T(8,128)}, u32[]{:S(2)}) copy-start(f32[64,64,64]{0,1,2:T(8,128)} %copy.212) | copy-start | bytes 3145732
  348.8 8.4 copy-start.25
  348.8 8.4 copy-start.26
  353.8 3.4 copy-start.22
  353.8 3.4 copy-start.23
  353.8 3.4 copy-start.24
  377.1 3.6 copy-start.1
  386.7 30.3 %all-to-all-start.7 = ((f32[1,1,1,128,4,8,128]{3,6,5,2,1,0,4:T(8,128)}), f32[1,1,1,128,4,8,128]{3,6,5,2,1,0,4:T(8,128)}, u32[]{:S(2)}, u32[]{:S(2)}) async-start(f32[1,1,1,128,4,8,128]{3,6,5,2,1,0,4:T(8,128)} %bitcast.454), calls=%async_computation.7 | async-start | bytes 4194304 | tf_op jit(solution)/shard_map/all_to_all | solution.py:102
  417.0 28.6 %all-to-all-start.5 = ((f32[1,1,1,128,4,8,128]{3,6,5,2,1,0,4:T(8,128)}), f32[1,1,1,128,4,8,128]{3,6,5,2,1,0,4:T(8,128)S(1)}, u32[]{:S(2)}, u32[]{:S(2)}) async-start(f32[1,1,1,128,4,8,128]{3,6,5,2,1,0,4:T(8,128)} %bitcast.455), calls=%async_computation.5 | async-start | bytes 4194304 | tf_op jit(solution)/shard_map/all_to_all | solution.py:95
  445.6 53.5 %all-to-all-start.8 = ((f32[1,4,1,128,1,8,128]{3,6,1,4,2,0,5:T(8,128)}), f32[1,4,1,128,1,8,128]{3,6,1,4,2,0,5:T(8,128)}, u32[]{:S(2)}, u32[]{:S(2)}) async-start(f32[1,4,1,128,1,8,128]{3,6,1,4,2,0,5:T(8,128)} %copy.226), calls=%async_computation.8 | async-start | bytes 4194304 | tf_op jit(solution)/shard_map/all_to_all | solution.py:101
  451.5 52.4 %copy-start.5 = (f32[128,64,64]{0,1,2:T(8,128)S(1)}, f32[128,64,64]{0,1,2:T(8,128)}, u32[]{:S(2)}) copy-start(f32[128,64,64]{0,1,2:T(8,128)} %get-tuple-element.22) | copy-start | bytes 6291460
  499.1 53.8 %all-to-all-start.6 = ((f32[1,4,1,128,1,8,128]{3,6,1,4,2,0,5:T(8,128)}), f32[1,4,1,128,1,8,128]{3,6,1,4,2,0,5:T(8,128)}, u32[]{:S(2)}, u32[]{:S(2)}) async-start(f32[1,4,1,128,1,8,128]{3,6,1,4,2,0,5:T(8,128)} %copy.219), calls=%async_computation.6 | async-start | bytes 4194304 | tf_op jit(solution)/shard_map/all_to_all | solution.py:94
  503.9 2.2 copy-start.7
  560.8 5.1 copy-start.14
  566.0 3.4 copy-start.6
  566.0 3.4 copy-start.11
  566.0 3.4 copy-start.13
  575.5 3.4 copy-start
  584.8 29.9 %all-to-all-start.10 = ((f32[1,1,1,128,4,8,128]{3,6,5,2,1,0,4:T(8,128)}), f32[1,1,1,128,4,8,128]{3,6,5,2,1,0,4:T(8,128)}, u32[]{:S(2)}, u32[]{:S(2)}) async-start(f32[1,1,1,128,4,8,128]{3,6,5,2,1,0,4:T(8,128)} %bitcast.456), calls=%async_computation.10 | async-start | bytes 4194304 | tf_op jit(solution)/shard_map/all_to_all | solution.py:95
  614.8 28.0 %all-to-all-start.12 = ((f32[1,1,1,128,4,8,128]{3,6,5,2,1,0,4:T(8,128)}), f32[1,1,1,128,4,8,128]{3,6,5,2,1,0,4:T(8,128)S(1)}, u32[]{:S(2)}, u32[]{:S(2)}) async-start(f32[1,1,1,128,4,8,128]{3,6,5,2,1,0,4:T(8,128)} %bitcast.457), calls=%async_computation.12 | async-start | bytes 4194304 | tf_op jit(solution)/shard_map/all_to_all | solution.py:102
  642.7 53.4 %all-to-all-start.11 = ((f32[1,4,1,128,1,8,128]{3,6,1,4,2,0,5:T(8,128)}), f32[1,4,1,128,1,8,128]{3,6,1,4,2,0,5:T(8,128)}, u32[]{:S(2)}, u32[]{:S(2)}) async-start(f32[1,4,1,128,1,8,128]{3,6,1,4,2,0,5:T(8,128)} %copy.246), calls=%async_computation.11 | async-start | bytes 4194304 | tf_op jit(solution)/shard_map/all_to_all | solution.py:94
  648.6 52.1 %copy-start.12 = (f32[128,64,64]{0,1,2:T(8,128)S(1)}, f32[128,64,64]{0,1,2:T(8,128)}, u32[]{:S(2)}) copy-start(f32[128,64,64]{0,1,2:T(8,128)} %get-tuple-element.10) | copy-start | bytes 6291460
  696.2 53.6 %all-to-all-start.13 = ((f32[1,4,1,128,1,8,128]{3,6,1,4,2,0,5:T(8,128)}), f32[1,4,1,128,1,8,128]{3,6,1,4,2,0,5:T(8,128)}, u32[]{:S(2)}, u32[]{:S(2)}) async-start(f32[1,4,1,128,1,8,128]{3,6,1,4,2,0,5:T(8,128)} %copy.253), calls=%async_computation.13 | async-start | bytes 4194304 | tf_op jit(solution)/shard_map/all_to_all | solution.py:101
  700.7 3.4 copy-start.10
  749.8 54.4 %all-to-all-start.9 = ((f32[1,128,4096]{1,0,2:T(1,128)}), f32[1,128,4096]{1,0,2:T(1,128)}, u32[]{:S(2)}, u32[]{:S(2)}) async-start(f32[1,128,4096]{1,0,2:T(1,128)} %bitcast.95), calls=%async_computation.9 | async-start | bytes 4194304 | tf_op jit(solution)/shard_map/all_to_all | solution.py:209
  778.3 5.0 copy-start.2
  804.2 54.1 %all-to-all-start.14 = ((f32[1,128,4096]{1,0,2:T(1,128)}), f32[1,128,4096]{1,0,2:T(1,128)S(1)}, u32[]{:S(2)}, u32[]{:S(2)}) async-start(f32[1,128,4096]{1,0,2:T(1,128)} %bitcast.154), calls=%async_computation.14 | async-start | bytes 4194304 | tf_op jit(solution)/shard_map/all_to_all | solution.py:209
where the time goes:
time: 880 us; the launch traced here: 865 us
  waiting for transfers between devices  346 us (39%)
  local copies, waits for them, and re-layouts  265 us (30%)
  matrix products  168 us (19%)
  starting transfers between devices  68.2 us (8%)
  other arithmetic  17.4 us (2%)
    dot_general x42, matrix products, contract(): jnp.einsum(pattern, table, values, precision=lax.Precision.HIGHEST, prefe...  168 us
    all_to_all x2, waiting for transfers between devices, to_spatial(): lax.all_to_all(lax.all_to_all(imag_part, 'grp', split_axis=4, concat_axis...  87.3 us
    all_to_all x2, waiting for transfers between devices, to_spatial(): lax.all_to_all(lax.all_to_all(real_part, 'grp', split_axis=4, concat_axis...  70.3 us
    unnamed x80, local copies, waits for them, and re-layouts  68.4 us
    all_to_all x1, waiting for transfers between devices, body(): lax.all_to_all(boundary_heat_flux, 'dev', split_axis=0, concat_axis=1, ti...  48.6 us
    all_to_all x2, waiting for transfers between devices, finish(): lax.all_to_all(rows_done, 'dev', split_axis=2, concat_axis=1, tiled=True)  46.1 us
    all_to_all x2, waiting for transfers between devices, to_spatial(): lax.all_to_all(imag_part, 'grp', split_axis=4, concat_axis=1, tiled=True)  36.2 us
    all_to_all x2, waiting for transfers between devices, to_spatial(): lax.all_to_all(real_part, 'grp', split_axis=4, concat_axis=1, tiled=True)  36 us
  transfers between devices with their start and end apart: 15, of which 11 were waited for; matrix products, arithmetic and copies ran while one was open for 36% of the time, Pallas kernels for 0%

commit v1 on v0

--- a/solution.py
+++ b/solution.py
@@ -1,8 +1,12 @@
+import functools
 import math
 
 import jax
 import jax.numpy as jnp
+import numpy as np
 from jax import lax
+from jax.experimental import pallas as pl
+from jax.experimental.pallas import tpu as pltpu
 from jax.sharding import PartitionSpec as P
 
 
@@ -218,8 +222,445 @@
     return thermal_rise
 
 
+MESH = pl.DeviceIdType.MESH
+RADIX = 8
+LANES = 128
+VMEM_LIMIT = 56 * 1024 * 1024
+HALF_ROOT = math.sqrt(0.5)
+
+
+def high_low(values):
+    high = values.astype(jnp.bfloat16)
+    return high, (values - high.astype(jnp.float32)).astype(jnp.bfloat16)
+
+
+def split_table(table):
+    table = np.asarray(table, np.float32)
+    high = table.astype(jnp.bfloat16)
+    low = (table - high.astype(np.float32)).astype(jnp.bfloat16)
+    return jnp.asarray(np.stack([high, low]))
+
+
+def complex_table(rows, columns, length, direction):
+    angle = (np.outer(np.arange(rows), np.arange(columns)) % length) * (2.0 * np.pi / length)
+    cos, sin = np.cos(angle), direction * np.sin(angle)
+    return np.concatenate(
+        [np.concatenate([cos, sin], axis=1), np.concatenate([-sin, cos], axis=1)], axis=0
+    )
+
+
+def twiddle_table(points, length, direction):
+    angle = (np.outer(np.arange(RADIX), np.arange(points)) % length) * (2.0 * np.pi / length)
+    return jnp.asarray(
+        np.stack([np.cos(angle), direction * np.sin(angle)], axis=1).astype(np.float32)
+    )
+
+
+def add(a, b):
+    return (a[0] + b[0], a[1] + b[1])
+
+
+def sub(a, b):
+    return (a[0] - b[0], a[1] - b[1])
+
+
+def times(a, b):
+    return (a[0] * b[0] - a[1] * b[1], a[0] * b[1] + a[1] * b[0])
+
+
+def quarter(a, direction):
+    return (-a[1], a[0]) if direction > 0 else (a[1], -a[0])
+
+
+def eighth(a, direction):
+    if direction > 0:
+        return ((a[0] - a[1]) * HALF_ROOT, (a[0] + a[1]) * HALF_ROOT)
+    return ((a[0] + a[1]) * HALF_ROOT, (a[1] - a[0]) * HALF_ROOT)
+
+
+def four_point(a, direction):
+    e0, e1 = add(a[0], a[2]), sub(a[0], a[2])
+    o0, o1 = add(a[1], a[3]), quarter(sub(a[1], a[3]), direction)
+    return [add(e0, o0), add(e1, o1), sub(e0, o0), sub(e1, o1)]
+
+
+def eight_point(a, direction):
+    even = four_point(a[0::2], direction)
+    odd = four_point(a[1::2], direction)
+    odd = [
+        odd[0],
+        eighth(odd[1], direction),
+        quarter(odd[2], direction),
+        quarter(eighth(odd[3], direction), direction),
+    ]
+    return [add(e, o) for e, o in zip(even, odd)] + [sub(e, o) for e, o in zip(even, odd)]
+
+
+def eight_point_of_real(a):
+    s0, d0 = a[0] + a[4], a[0] - a[4]
+    s1, d1 = a[1] + a[5], a[1] - a[5]
+    s2, d2 = a[2] + a[6], a[2] - a[6]
+    s3, d3 = a[3] + a[7], a[3] - a[7]
+    p, q = (d1 - d3) * HALF_ROOT, (d1 + d3) * HALF_ROOT
+    zero = jnp.zeros_like(s0)
+    x1 = (d0 + p, -d2 - q)
+    x3 = (d0 - p, d2 - q)
+    x2 = (s0 - s2, s3 - s1)
+    ev, od = s0 + s2, s1 + s3
+    conj = lambda z: (z[0], -z[1])
+    return [(ev + od, zero), x1, x2, x3, (ev - od, zero), conj(x3), conj(x2), conj(x1)]
+
+
+def eight_point_to_real(b):
+    c1, c2, c3 = [(b[i][0] + b[8 - i][0], b[i][1] - b[8 - i][1]) for i in (1, 2, 3)]
+    p, m = b[0][0] + b[4][0], b[0][0] - b[4][0]
+    e0, e2 = p + c2[0], p - c2[0]
+    e1, e3 = m - c2[1], m + c2[1]
+    o0 = c1[0] + c3[0]
+    o2 = c3[1] - c1[1]
+    o1 = (c1[0] - c1[1] - c3[0] - c3[1]) * HALF_ROOT
+    o3 = (c3[0] - c3[1] - c1[0] - c1[1]) * HALF_ROOT
+    return [e0 + o0, e1 + o1, e2 + o2, e3 + o3, e0 - o0, e1 - o1, e2 - o2, e3 - o3]
+
+
+def three_products(high, low, table_high, table_low):
+    dot = functools.partial(jnp.dot, preferred_element_type=jnp.float32)
+    return dot(high, table_high) + dot(high, table_low) + dot(low, table_high)
+
+
+def exchange_kernel(counts, whole, src, dst, send_sem, recv_sem, own_sem):
+    groups, members = counts
+    grp, dev = lax.axis_index("grp"), lax.axis_index("dev")
+    count = groups * members if whole else members
+    me = grp * members + dev if whole else dev
+
+    def place(pos):
+        return (pos // members, pos % members) if whole else (grp, pos)
+
+    barrier = pltpu.get_barrier_semaphore()
+    for offset in range(1, count):
+        pl.semaphore_signal(
+            barrier, inc=1, device_id=place((me + offset) % count), device_id_type=MESH
+        )
+    pl.semaphore_wait(barrier, count - 1)
+
+    def copy(offset, source, target):
+        return pltpu.make_async_remote_copy(
+            src_ref=src.at[target],
+            dst_ref=dst.at[source],
+            send_sem=send_sem.at[offset],
+            recv_sem=recv_sem.at[offset],
+            device_id=place(target),
+            device_id_type=MESH,
+        )
+
+    for offset in range(1, count):
+        copy(offset, me, (me + offset) % count).start()
+    own = pltpu.make_async_copy(src.at[me], dst.at[me], own_sem)
+    own.start()
+    own.wait()
+    for offset in range(1, count):
+        copy(offset, me, (me + offset) % count).wait_send()
+        copy(offset, (me + count - offset) % count, (me + offset) % count).wait_recv()
+
+
+def exchange(values, counts, whole, collective_id):
+    count = values.shape[0]
+    return pl.pallas_call(
+        functools.partial(exchange_kernel, counts, whole),
+        out_shape=jax.ShapeDtypeStruct(values.shape, values.dtype),
+        in_specs=[pl.BlockSpec(memory_space=pl.ANY)],
+        out_specs=pl.BlockSpec(memory_space=pl.ANY),
+        scratch_shapes=[
+            pltpu.SemaphoreType.DMA((count,)),
+            pltpu.SemaphoreType.DMA((count,)),
+            pltpu.SemaphoreType.DMA,
+        ],
+        compiler_params=pltpu.CompilerParams(collective_id=collective_id, has_side_effects=True),
+    )(values)
+
+
+def forward_y_kernel(flux, table, twiddle, out, high, low):
+    members, x_rows, trail = flux.shape
+    count, _, block_rows, _ = out.shape
+    sub_rows = block_rows // RADIX
+
+    @pl.loop(0, x_rows // 16)
+    def _(chunk):
+        rows = pl.ds(pl.multiple_of(chunk * 16, 16), 16)
+        for lane in range(trail // LANES):
+            lanes = slice(lane * LANES, (lane + 1) * LANES)
+            parts = eight_point_of_real([flux[s, rows, lanes] for s in range(RADIX)])
+            for v0 in range(RADIX):
+                real, imag = times(
+                    parts[v0], (twiddle[v0, 0:1, lanes], twiddle[v0, 1:2, lanes])
+                )
+                for part, value in enumerate((real, imag)):
+                    to = slice(part * trail + lane * LANES, part * trail + (lane + 1) * LANES)
+                    hi, lo = high_low(value)
+                    high[v0, rows, to] = hi
+                    low[v0, rows, to] = lo
+
+    @pl.loop(0, RADIX // 2)
+    def _(pair):
+        hi = high[pl.ds(pair * 2, 2)].reshape(2 * x_rows, 2 * trail)
+        lo = low[pl.ds(pair * 2, 2)].reshape(2 * x_rows, 2 * trail)
+
+        def dot(a, b):
+            return lax.dot_general(
+                a, b, (((1,), (1,)), ((), ())), preferred_element_type=jnp.float32
+            )
+
+        half = table.shape[1] // 2
+        for part in range(2):
+            t_hi = table[0, part * half : (part + 1) * half]
+            t_lo = table[1, part * half : (part + 1) * half]
+            result = dot(t_hi, hi) + dot(t_lo, hi) + dot(t_hi, lo)
+            for side in range(2):
+                piece = result[:, side * x_rows : (side + 1) * x_rows]
+                piece = piece.reshape(count, sub_rows, x_rows)
+                for k in range(count):
+                    out[k, part, pl.ds(pair * 2 + side, sub_rows, stride=RADIX), :] = piece[k]
+
+
+def middle_kernel(recv, kernel_ref, weight, table_in, table_out, twiddle, out, hi_a, lo_a, mid, hi_b, lo_b):
+    count, _, block_rows, x_rows = recv.shape
+    layers = kernel_ref.shape[0]
+    groups = count // RADIX
+    points = groups * x_rows
+    rows_all = RADIX * block_rows
+
+    @pl.loop(0, RADIX)
+    def _(d):
+        for g in range(groups):
+            for part in range(2):
+                to = slice(part * points + g * x_rows, part * points + (g + 1) * x_rows)
+                hi, lo = high_low(recv[g * RADIX + d, part])
+                hi_a[d, :, to] = hi
+                lo_a[d, :, to] = lo
+
+    tiles, _, width = table_in.shape[1:]
+
+    @pl.loop(0, tiles)
+    def _(n):
+        result = three_products(
+            hi_a[...].reshape(rows_all, 2 * points),
+            lo_a[...].reshape(rows_all, 2 * points),
+            table_in[0, n],
+            table_in[1, n],
+        )
+        mid[n] = result.reshape(RADIX, block_rows, width)
+
+    @pl.loop(0, block_rows // 16)
+    def _(chunk):
+        rows = pl.ds(pl.multiple_of(chunk * 16, 16), 16)
+        scale = weight[rows, :]
+        for lane in range(points // LANES):
+            column = lane * LANES
+            lanes = slice(column, column + LANES)
+            within = slice(column % width, column % width + LANES)
+            tile = column // width
+            turn = [(twiddle[d, 0:1, lanes], twiddle[d, 1:2, lanes]) for d in range(RADIX)]
+            spec = eight_point(
+                [
+                    times(
+                        (mid[tile, d, rows, within], mid[tile + tiles // 2, d, rows, within]),
+                        turn[d],
+                    )
+                    for d in range(RADIX)
+                ],
+                -1.0,
+            )
+            spec = [(a * scale, b * scale) for a, b in spec]
+            for layer in range(layers):
+                prod = []
+                for u2 in range(RADIX):
+                    at = slice(u2 * points + column, u2 * points + column + LANES)
+                    prod.append(
+                        times(spec[u2], (kernel_ref[layer, 0, rows, at], kernel_ref[layer, 1, rows, at]))
+                    )
+                back = eight_point(prod, 1.0)
+                for d in range(RADIX):
+                    both = times(back[d], (turn[d][0], -turn[d][1]))
+                    for part in range(2):
+                        to = slice(part * points + column, part * points + column + LANES)
+                        hi, lo = high_low(both[part])
+                        hi_b[layer, d, rows, to] = hi
+                        lo_b[layer, d, rows, to] = lo
+
+    for layer in range(layers):
+
+        @pl.loop(0, tiles)
+        def _(n):
+            result = three_products(
+                hi_b[layer].reshape(rows_all, 2 * points),
+                lo_b[layer].reshape(rows_all, 2 * points),
+                table_out[0, n],
+                table_out[1, n],
+            ).reshape(RADIX, block_rows, width)
+            part = n // (tiles // 2)
+            first = (n % (tiles // 2)) * (width // x_rows)
+            for side in range(width // x_rows):
+                for d in range(RADIX):
+                    out[(first + side) * RADIX + d, layer, part] = result[
+                        d, :, side * x_rows : (side + 1) * x_rows
+                    ]
+
+
+def inverse_y_kernel(recv, table, twiddle, out, high, low, mid):
+    count, _, block_rows, x_rows = recv.shape
+    sub_rows = block_rows // RADIX
+    depth = count * sub_rows
+
+    @pl.loop(0, RADIX)
+    def _(v0):
+        for part in range(2):
+            pieces = [
+                recv[k, part, pl.ds(v0, sub_rows, stride=RADIX), :] for k in range(count)
+            ]
+            turned = jnp.concatenate(pieces, axis=0).T
+            hi, lo = high_low(turned)
+            high[v0, :, part * depth : (part + 1) * depth] = hi
+            low[v0, :, part * depth : (part + 1) * depth] = lo
+
+    tiles, _, width = table.shape[1:]
+
+    @pl.loop(0, tiles)
+    def _(n):
+        result = three_products(
+            high[...].reshape(RADIX * x_rows, 2 * depth),
+            low[...].reshape(RADIX * x_rows, 2 * depth),
+            table[0, n],
+            table[1, n],
+        )
+        mid[n] = result.reshape(RADIX, x_rows, width)
+
+    trail = out.shape[-1]
+
+    @pl.loop(0, x_rows // 8)
+    def _(chunk):
+        rows = pl.ds(pl.multiple_of(chunk * 8, 8), 8)
+        for lane in range(trail // LANES):
+            column = lane * LANES
+            lanes = slice(column, column + LANES)
+            within = slice(column % width, column % width + LANES)
+            tile = column // width
+            result = eight_point_to_real(
+                [
+                    times(
+                        (mid[tile, v, rows, within], mid[tile + tiles // 2, v, rows, within]),
+                        (twiddle[v, 0:1, lanes], twiddle[v, 1:2, lanes]),
+                    )
+                    for v in range(RADIX)
+                ]
+            )
+            for s in range(RADIX):
+                out[s, rows, lanes] = result[s]
+
+
+def tile_columns(table, width):
+    rows, columns = table.shape
+    return table.reshape(rows, columns // width, width).transpose(1, 0, 2)
+
+
+def vmem_call(kernel, out_shape, scratch, *operands):
+    return pl.pallas_call(
+        kernel,
+        out_shape=jax.ShapeDtypeStruct(out_shape, jnp.float32),
+        in_specs=[pl.BlockSpec(memory_space=pltpu.VMEM)] * len(operands),
+        out_specs=pl.BlockSpec(memory_space=pltpu.VMEM),
+        scratch_shapes=[pltpu.VMEM(shape, dtype) for shape, dtype in scratch],
+        compiler_params=pltpu.CompilerParams(vmem_limit_bytes=VMEM_LIMIT),
+    )(*operands)
+
+
+def fast_body(boundary_heat_flux, layer_kernel):
+    groups, members = lax.axis_size("grp"), lax.axis_size("dev")
+    counts = (groups, members)
+    count = groups * members
+    local_x, trail = boundary_heat_flux.shape
+    x_rows = local_x // members
+    layers, _, block_rows, width_x = layer_kernel.shape
+    width_y = trail * members
+    half = block_rows * count // RADIX
+    points = width_x // RADIX
+    bf16, f32 = jnp.bfloat16, jnp.float32
+    device_pos = lax.axis_index("grp") * members + lax.axis_index("dev")
+    first = jnp.logical_and(device_pos == 0, lax.broadcasted_iota(jnp.int32, (block_rows, LANES), 0) == 0)
+    weight = jnp.where(first, 1.0, 2.0).astype(f32) * (1.0 / (width_x * width_y))
+
+    table_fy = split_table(complex_table(trail, half, trail, -1.0).T)
+    table_in = split_table(tile_columns(complex_table(points, points, points, -1.0), 256))
+    table_out = split_table(tile_columns(complex_table(points, points, points, 1.0), 256))
+    table_iy = split_table(tile_columns(complex_table(half, trail, trail, 1.0), 256))
+    twiddle_fy = twiddle_table(trail, width_y, -1.0)
+    twiddle_x = twiddle_table(points, width_x, -1.0)
+    twiddle_iy = twiddle_table(trail, width_y, 1.0)
+
+    sent = boundary_heat_flux.reshape(x_rows, members, trail).transpose(1, 0, 2)
+    flux = exchange(sent, counts, False, 0)
+    spec = vmem_call(
+        forward_y_kernel,
+        (count, 2, block_rows, x_rows),
+        [((RADIX, x_rows, 2 * trail), bf16)] * 2,
+        flux,
+        table_fy,
+        twiddle_fy,
+    )
+    spec = exchange(spec, counts, True, 1)
+    back = vmem_call(
+        middle_kernel,
+        (count, layers, 2, block_rows, x_rows),
+        [((RADIX, block_rows, 2 * points), bf16)] * 2
+        + [((2 * points // 256, RADIX, block_rows, 256), f32)]
+        + [((layers, RADIX, block_rows, 2 * points), bf16)] * 2,
+        spec,
+        layer_kernel,
+        weight,
+        table_in,
+        table_out,
+        twiddle_x,
+    )
+    back = exchange(back, counts, True, 2)
+    rows = pl.pallas_call(
+        inverse_y_kernel,
+        grid=(layers,),
+        out_shape=jax.ShapeDtypeStruct((members, layers, x_rows, trail), f32),
+        in_specs=[
+            pl.BlockSpec((count, None, 2, block_rows, x_rows), lambda l: (0, l, 0, 0, 0)),
+            pl.BlockSpec(table_iy.shape, lambda l: (0, 0, 0, 0)),
+            pl.BlockSpec(twiddle_iy.shape, lambda l: (0, 0, 0)),
+        ],
+        out_specs=pl.BlockSpec((members, None, x_rows, trail), lambda l: (0, l, 0, 0)),
+        scratch_shapes=[
+            pltpu.VMEM((RADIX, x_rows, 2 * half), bf16),
+            pltpu.VMEM((RADIX, x_rows, 2 * half), bf16),
+            pltpu.VMEM((2 * trail // 256, RADIX, x_rows, 256), f32),
+        ],
+        compiler_params=pltpu.CompilerParams(vmem_limit_bytes=VMEM_LIMIT),
+    )(back, table_iy, twiddle_iy)
+    rows = exchange(rows, counts, False, 3)
+    return rows.transpose(1, 2, 0, 3).reshape(layers, local_x, trail)
+
+
 def solution(mesh):
     placed = (P("grp", "dev"), P(None, None, ("grp", "dev"), None))
+    groups, members = mesh.shape["grp"], mesh.shape["dev"]
+
+    def chosen(boundary_heat_flux, layer_kernel):
+        local_x, trail = boundary_heat_flux.shape
+        block_rows = layer_kernel.shape[2]
+        fits = (
+            members == RADIX
+            and local_x // members == LANES
+            and trail % LANES == 0
+            and groups * LANES * RADIX == layer_kernel.shape[3]
+            and block_rows % 16 == 0
+            and (groups * LANES) % 256 == 0
+            and trail % 256 == 0
+        )
+        return (fast_body if fits else body)(boundary_heat_flux, layer_kernel)
+
     return jax.shard_map(
-        body, mesh=mesh, in_specs=placed, out_specs=P(None, "grp", "dev"), check_vma=False
-    )
+        chosen, mesh=mesh, in_specs=placed, out_specs=P(None, "grp", "dev"), check_vma=False
+    )

time: 880 us -> 350 us (0.40)
  the two profiles are of different devices: /device:TPU:0 before, /device:TPU:9 now
where the time goes in v1:
time: 350 us
  Pallas kernels  338 us (97%)
  local copies, waits for them, and re-layouts  11.4 us (3%)
    pallas_call x4, Pallas kernels, exchange(): pl.pallas_call(functools.partial(exchange_kernel, counts, whole), out_sha...  292 us
    pallas_call x2, Pallas kernels, vmem_call(): pl.pallas_call(kernel, out_shape=jax.ShapeDtypeStruct(out_shape, jnp.floa...  31.1 us
    pallas_call x1, Pallas kernels, fast_body(): pl.pallas_call(inverse_y_kernel, grid=(layers,), out_shape=jax.ShapeDtype...  15.4 us

profile of v1, /device:TPU:9, one launch (start us, length us, event | category | flops | bytes accessed | tf_op | source)
XLA Modules:
  0.0 349.8 jit_solution(3430672809232838847)
XLA Ops:
  0.0 0.7 iota.7.weight
  0.7 4.1 %copy.15 = f32[128,8,512]{2,0,1:T(8,128)} copy(f32[128,8,512]{2,1,0:T(8,128)} %bitcast.10) | data formatting | bytes 4194304 | tf_op jit(solution)/shard_map/reshape | solution.py:600
  4.8 49.5 %shard_map.91.flux = f32[8,128,512]{2,1,0:T(8,128)} custom-call(f32[8,128,512]{2,1,0:T(8,128)} %bitcast.9), custom_call_target="tpu_custom_call" | custom-call | tf_op jit(solution)/shard_map/pallas_call | solution.py:369
  54.3 9.1 %shard_map.92.src = f32[32,2,64,128]{3,2,1,0:T(8,128)} custom-call(f32[8,128,512]{2,1,0:T(8,128)} %shard_map.91.flux, bf16[2,512,1024]{2,1,0:T(8,128)(2,1)} %constant.31.clone.table, f32[8,2,512]{2,1,0:T(2,128)} %constant.35.clone.twiddle), custom_call_target="tpu_custom_call" | custom-call | tf_op jit(solution)/shard_map/pallas_call | solution.py:567
  63.4 51.3 %shard_map.93.recv = f32[32,2,64,128]{3,2,1,0:T(8,128)} custom-call(f32[32,2,64,128]{3,2,1,0:T(8,128)} %shard_map.92.src), custom_call_target="tpu_custom_call" | custom-call | tf_op jit(solution)/shard_map/pallas_call | solution.py:369
  114.7 22.0 %shard_map.94.src = f32[32,2,2,64,128]{4,3,2,1,0:T(8,128)} custom-call(f32[32,2,64,128]{3,2,1,0:T(8,128)} %shard_map.93.recv, f32[2,2,64,4096]{3,2,1,0:T(8,128)} %kernel_ref.1, f32[64,128]{1,0:T(8,128)} %iota.7.weight, bf16[2,4,1024,256]{3,2,1,0:T(8,128)(2,1)} %constant.32.clone.table_in, bf16[2,4,1024,256]{3,2,1,0:T(8,128)(2,1)} %constant.33.clone.table_out, ...), custom_call_target="tpu_custom_call" | custom-call | tf_op jit(solution)/shard_map/pallas_call | solution.py:567
  136.7 96.1 %shard_map.95.recv = f32[32,2,2,64,128]{4,3,2,1,0:T(8,128)} custom-call(f32[32,2,2,64,128]{4,3,2,1,0:T(8,128)} %shard_map.94.src), custom_call_target="tpu_custom_call" | custom-call | tf_op jit(solution)/shard_map/pallas_call | solution.py:369
  232.7 15.4 %shard_map.96.src = f32[8,2,128,512]{3,2,1,0:T(8,128)} custom-call(f32[32,2,2,64,128]{4,3,2,1,0:T(8,128)} %shard_map.95.recv, bf16[2,4,512,256]{3,2,1,0:T(8,128)(2,1)} %constant.34.clone.table, f32[8,2,512]{2,1,0:T(2,128)} %constant.36.clone.twiddle), custom_call_target="tpu_custom_call" | custom-call | tf_op jit(solution)/shard_map/pallas_call | solution.py:625
  248.1 95.1 %shard_map.97 = f32[8,2,128,512]{3,2,1,0:T(8,128)} custom-call(f32[8,2,128,512]{3,2,1,0:T(8,128)} %shard_map.96.src), custom_call_target="tpu_custom_call" | custom-call | tf_op jit(solution)/shard_map/pallas_call | solution.py:369
  343.2 6.6 %copy.14 = f32[2,128,8,512]{3,2,1,0:T(8,128)} copy(f32[2,128,8,512]{3,1,0,2:T(8,128)} %bitcast.8) | data formatting | bytes 8388608 | tf_op jit(solution)/shard_map/transpose | solution.py:643
  (1 shorter events, 0.0 us)

commit v2 on v0

--- a/solution.py
+++ b/solution.py
@@ -1,8 +1,12 @@
+import functools
 import math
 
 import jax
 import jax.numpy as jnp
+import numpy as np
 from jax import lax
+from jax.experimental import pallas as pl
+from jax.experimental.pallas import tpu as pltpu
 from jax.sharding import PartitionSpec as P
 
 
@@ -218,8 +222,563 @@
     return thermal_rise
 
 
+MESH = pl.DeviceIdType.MESH
+RADIX = 8
+LANES = 128
+VMEM_LIMIT = 56 * 1024 * 1024
+HALF_ROOT = math.sqrt(0.5)
+
+
+def high_low(values):
+    high = values.astype(jnp.bfloat16)
+    return high, (values - high.astype(jnp.float32)).astype(jnp.bfloat16)
+
+
+def split_table(table):
+    table = np.asarray(table, np.float32)
+    high = table.astype(jnp.bfloat16)
+    low = (table - high.astype(np.float32)).astype(jnp.bfloat16)
+    return jnp.asarray(np.stack([high, low]))
+
+
+def complex_table(rows, columns, length, direction):
+    angle = (np.outer(np.arange(rows), np.arange(columns)) % length) * (2.0 * np.pi / length)
+    cos, sin = np.cos(angle), direction * np.sin(angle)
+    return np.concatenate(
+        [np.concatenate([cos, sin], axis=1), np.concatenate([-sin, cos], axis=1)], axis=0
+    )
+
+
+def twiddle_table(points, length, direction):
+    angle = (np.outer(np.arange(RADIX), np.arange(points)) % length) * (2.0 * np.pi / length)
+    return jnp.asarray(
+        np.stack([np.cos(angle), direction * np.sin(angle)], axis=1).astype(np.float32)
+    )
+
+
+def add(a, b):
+    return (a[0] + b[0], a[1] + b[1])
+
+
+def sub(a, b):
+    return (a[0] - b[0], a[1] - b[1])
+
+
+def times(a, b):
+    return (a[0] * b[0] - a[1] * b[1], a[0] * b[1] + a[1] * b[0])
+
+
+def quarter(a, direction):
+    return (-a[1], a[0]) if direction > 0 else (a[1], -a[0])
+
+
+def eighth(a, direction):
+    if direction > 0:
+        return ((a[0] - a[1]) * HALF_ROOT, (a[0] + a[1]) * HALF_ROOT)
+    return ((a[0] + a[1]) * HALF_ROOT, (a[1] - a[0]) * HALF_ROOT)
+
+
+def four_point(a, direction):
+    e0, e1 = add(a[0], a[2]), sub(a[0], a[2])
+    o0, o1 = add(a[1], a[3]), quarter(sub(a[1], a[3]), direction)
+    return [add(e0, o0), add(e1, o1), sub(e0, o0), sub(e1, o1)]
+
+
+def eight_point(a, direction):
+    even = four_point(a[0::2], direction)
+    odd = four_point(a[1::2], direction)
+    odd = [
+        odd[0],
+        eighth(odd[1], direction),
+        quarter(odd[2], direction),
+        quarter(eighth(odd[3], direction), direction),
+    ]
+    return [add(e, o) for e, o in zip(even, odd)] + [sub(e, o) for e, o in zip(even, odd)]
+
+
+def eight_point_of_real(a):
+    s0, d0 = a[0] + a[4], a[0] - a[4]
+    s1, d1 = a[1] + a[5], a[1] - a[5]
+    s2, d2 = a[2] + a[6], a[2] - a[6]
+    s3, d3 = a[3] + a[7], a[3] - a[7]
+    p, q = (d1 - d3) * HALF_ROOT, (d1 + d3) * HALF_ROOT
+    zero = jnp.zeros_like(s0)
+    x1 = (d0 + p, -d2 - q)
+    x3 = (d0 - p, d2 - q)
+    x2 = (s0 - s2, s3 - s1)
+    ev, od = s0 + s2, s1 + s3
+    conj = lambda z: (z[0], -z[1])
+    return [(ev + od, zero), x1, x2, x3, (ev - od, zero), conj(x3), conj(x2), conj(x1)]
+
+
+def eight_point_to_real(b):
+    c1, c2, c3 = [(b[i][0] + b[8 - i][0], b[i][1] - b[8 - i][1]) for i in (1, 2, 3)]
+    p, m = b[0][0] + b[4][0], b[0][0] - b[4][0]
+    e0, e2 = p + c2[0], p - c2[0]
+    e1, e3 = m - c2[1], m + c2[1]
+    o0 = c1[0] + c3[0]
+    o2 = c3[1] - c1[1]
+    o1 = (c1[0] - c1[1] - c3[0] - c3[1]) * HALF_ROOT
+    o3 = (c3[0] - c3[1] - c1[0] - c1[1]) * HALF_ROOT
+    return [e0 + o0, e1 + o1, e2 + o2, e3 + o3, e0 - o0, e1 - o1, e2 - o2, e3 - o3]
+
+
+def three_products(high, low, table_high, table_low):
+    dot = functools.partial(jnp.dot, preferred_element_type=jnp.float32)
+    return dot(high, table_high) + dot(high, table_low) + dot(low, table_high)
+
+
+PARTS_IN = 4
+HALVES = 2
+
+
+def whole_kernel(
+    counts, flux, kernel_hbm, weight_hbm, fy_hbm, in_hbm, out_hbm, iy_hbm, tw_fy_hbm, tw_x_hbm, tw_iy_hbm,
+    result_hbm,
+    staged, send_rows, recv_rows, high, low, send_spec, recv_spec, hi_a, lo_a, mid_x, hi_b, lo_b,
+    send_back, recv_back, mid_y, kernel_ref, weight, table_fy, table_in, table_out, table_iy,
+    twiddle_fy, twiddle_x, twiddle_iy,
+    load_sem, stage_sem, a_send, a_recv, b_send, b_recv, b_own, c_send, c_recv, c_own, d_send, d_recv, d_own,
+    done_sem,
+):
+    groups, members = counts
+    count = groups * members
+    grp, dev = lax.axis_index("grp"), lax.axis_index("dev")
+    me = grp * members + dev
+    layers = kernel_ref.shape[0]
+    _, _, x_rows, trail = recv_rows.shape
+    part_rows = x_rows // PARTS_IN
+    half_rows = recv_spec.shape[3]
+    points = groups * x_rows
+    lane_blocks = trail // LANES
+    sub_rows = HALVES * half_rows // RADIX
+    depth = count * sub_rows
+
+    def stage(lane):
+        return pltpu.make_async_copy(
+            flux.at[:, pl.ds(lane * LANES, LANES)], staged.at[lane], stage_sem.at[lane]
+        )
+
+    for lane in range(lane_blocks):
+        stage(lane).start()
+    loads = [
+        pltpu.make_async_copy(a, b, load_sem.at[i])
+        for i, (a, b) in enumerate(
+            [
+                (tw_fy_hbm, twiddle_fy),
+                (fy_hbm, table_fy),
+                (in_hbm, table_in),
+                (kernel_hbm, kernel_ref),
+                (weight_hbm, weight),
+                (tw_x_hbm, twiddle_x),
+                (out_hbm, table_out),
+                (iy_hbm, table_iy),
+                (tw_iy_hbm, twiddle_iy),
+            ]
+        )
+    ]
+
+    barrier = pltpu.get_barrier_semaphore()
+
+    def place(pos):
+        return (lax.div(pos, members), lax.rem(pos, members))
+
+    @pl.loop(1, count)
+    def _(offset):
+        pl.semaphore_signal(
+            barrier, inc=1, device_id=place(lax.rem(me + offset, count)), device_id_type=MESH
+        )
+
+    for lane in range(lane_blocks):
+        stage(lane).wait()
+    for load in loads:
+        load.start()
+    pl.semaphore_wait(barrier, count - 1)
+
+    for part in range(PARTS_IN):
+        rows = pl.ds(part * part_rows, part_rows)
+
+        @pl.loop(1, members)
+        def _(offset):
+            target = lax.rem(dev + offset, members)
+            for lane in range(lane_blocks):
+                send_rows[0, target, rows, lane * LANES : (lane + 1) * LANES] = staged[
+                    lane, pl.ds(part * part_rows * members + target, part_rows, stride=members), :
+                ]
+            pltpu.make_async_remote_copy(
+                src_ref=send_rows.at[0, target, rows],
+                dst_ref=recv_rows.at[0, dev, rows],
+                send_sem=a_send.at[part],
+                recv_sem=a_recv.at[part],
+                device_id=(grp, target),
+                device_id_type=MESH,
+            ).start()
+
+        for lane in range(lane_blocks):
+            recv_rows[0, dev, rows, lane * LANES : (lane + 1) * LANES] = staged[
+                lane, pl.ds(part * part_rows * members + dev, part_rows, stride=members), :
+            ]
+
+    def wait_bytes(ref, sem):
+        pltpu.make_async_copy(ref, ref, sem).wait()
+
+    loads[0].wait()
+    for part in range(PARTS_IN):
+        wait_bytes(recv_rows.at[0, pl.ds(0, members - 1), pl.ds(part * part_rows, part_rows)], a_recv.at[part])
+
+        @pl.loop(0, part_rows // 16)
+        def _(chunk):
+            rows = pl.ds(pl.multiple_of(part * part_rows + chunk * 16, 16), 16)
+            for lane in range(lane_blocks):
+                lanes = slice(lane * LANES, (lane + 1) * LANES)
+                parts = eight_point_of_real([recv_rows[0, s, rows, lanes] for s in range(RADIX)])
+                for v0 in range(RADIX):
+                    pair = times(parts[v0], (twiddle_fy[v0, 0:1, lanes], twiddle_fy[v0, 1:2, lanes]))
+                    for side, value in enumerate(pair):
+                        to = slice(side * trail + lane * LANES, side * trail + (lane + 1) * LANES)
+                        hi, lo = high_low(value)
+                        high[v0, rows, to] = hi
+                        low[v0, rows, to] = lo
+
+    loads[1].wait()
+
+    def send_all(source, target_of, send_sem, recv_sem, own_sem):
+        @pl.loop(1, count)
+        def _(offset):
+            target = lax.rem(me + offset, count)
+            pltpu.make_async_remote_copy(
+                src_ref=source.at[target],
+                dst_ref=target_of(me),
+                send_sem=send_sem,
+                recv_sem=recv_sem,
+                device_id=place(target),
+                device_id_type=MESH,
+            ).start()
+
+        pltpu.make_async_copy(source.at[me], target_of(me), own_sem).start()
+
+    def dot_rows(a, b):
+        return lax.dot_general(a, b, (((1,), (1,)), ((), ())), preferred_element_type=jnp.float32)
+
+    quarter_rows = half_rows // RADIX
+    for half in range(HALVES):
+
+        @pl.loop(0, RADIX // 2)
+        def _(pair):
+            hi = high[pl.ds(pair * 2, 2)].reshape(2 * x_rows, 2 * trail)
+            lo = low[pl.ds(pair * 2, 2)].reshape(2 * x_rows, 2 * trail)
+            result = (
+                dot_rows(table_fy[0, half], hi)
+                + dot_rows(table_fy[1, half], hi)
+                + dot_rows(table_fy[0, half], lo)
+            )
+            for part in range(2):
+                for side in range(2):
+                    for k in range(count):
+                        at = (part * count + k) * quarter_rows
+                        send_spec[half, k, part, pl.ds(pair * 2 + side, quarter_rows, stride=RADIX), :] = result[
+                            at : at + quarter_rows, side * x_rows : (side + 1) * x_rows
+                        ]
+
+        send_all(
+            send_spec.at[half], lambda k: recv_spec.at[half, k], b_send.at[half], b_recv.at[half], b_own.at[half]
+        )
+
+    tiles, _, width = table_in.shape[1:]
+    rows_all = RADIX * half_rows
+    for load in loads[2:7]:
+        load.wait()
+    for half in range(HALVES):
+        wait_bytes(recv_spec.at[half, pl.ds(0, count - 1)], b_recv.at[half])
+        wait_bytes(recv_spec.at[half, 0], b_own.at[half])
+
+        @pl.loop(0, RADIX)
+        def _(d):
+            for g in range(groups):
+                for part in range(2):
+                    to = slice(part * points + g * x_rows, part * points + (g + 1) * x_rows)
+                    hi, lo = high_low(recv_spec[half, g * RADIX + d, part])
+                    hi_a[d, :, to] = hi
+                    lo_a[d, :, to] = lo
+
+        @pl.loop(0, tiles)
+        def _(n):
+            mid_x[n] = three_products(
+                hi_a[...].reshape(rows_all, 2 * points),
+                lo_a[...].reshape(rows_all, 2 * points),
+                table_in[0, n],
+                table_in[1, n],
+            ).reshape(RADIX, half_rows, width)
+
+        @pl.loop(0, half_rows // 16)
+        def _(chunk):
+            rows = pl.ds(pl.multiple_of(chunk * 16, 16), 16)
+            rows_of = pl.ds(pl.multiple_of(half * half_rows + chunk * 16, 16), 16)
+            scale = weight[rows_of, :]
+            for lane in range(points // LANES):
+                column = lane * LANES
+                lanes = slice(column, column + LANES)
+                within = slice(column % width, column % width + LANES)
+                tile = column // width
+                turn = [(twiddle_x[d, 0:1, lanes], twiddle_x[d, 1:2, lanes]) for d in range(RADIX)]
+                spec = eight_point(
+                    [
+                        times((mid_x[tile, d, rows, within], mid_x[tile + tiles // 2, d, rows, within]), turn[d])
+                        for d in range(RADIX)
+                    ],
+                    -1.0,
+                )
+                spec = [(a * scale, b * scale) for a, b in spec]
+                for layer in range(layers):
+                    prod = []
+                    for u2 in range(RADIX):
+                        at = slice(u2 * points + column, u2 * points + column + LANES)
+                        prod.append(
+                            times(spec[u2], (kernel_ref[layer, 0, rows_of, at], kernel_ref[layer, 1, rows_of, at]))
+                        )
+                    back = eight_point(prod, 1.0)
+                    for d in range(RADIX):
+                        both = times(back[d], (turn[d][0], -turn[d][1]))
+                        for part in range(2):
+                            to = slice(part * points + column, part * points + column + LANES)
+                            hi, lo = high_low(both[part])
+                            hi_b[layer, d, rows, to] = hi
+                            lo_b[layer, d, rows, to] = lo
+
+        for layer in range(layers):
+
+            @pl.loop(0, tiles)
+            def _(n):
+                result = three_products(
+                    hi_b[layer].reshape(rows_all, 2 * points),
+                    lo_b[layer].reshape(rows_all, 2 * points),
+                    table_out[0, n],
+                    table_out[1, n],
+                ).reshape(RADIX, half_rows, width)
+                part = n // (tiles // 2)
+                first = (n % (tiles // 2)) * (width // x_rows)
+                for side in range(width // x_rows):
+                    for d in range(RADIX):
+                        send_back[half, layer, (first + side) * RADIX + d, part] = result[
+                            d, :, side * x_rows : (side + 1) * x_rows
+                        ]
+
+            which = half * layers + layer
+            span = pl.ds(half * half_rows, half_rows)
+            send_all(
+                send_back.at[half, layer],
+                lambda k: recv_back.at[layer, k, :, span],
+                c_send.at[which],
+                c_recv.at[which],
+                c_own.at[which],
+            )
+
+    for part in range(PARTS_IN):
+        wait_bytes(send_rows.at[0, pl.ds(0, members - 1), pl.ds(part * part_rows, part_rows)], a_send.at[part])
+    for load in loads[7:]:
+        load.wait()
+    tiles_y, _, width_y = table_iy.shape[1:]
+
+    def rows_copy(layer, offset, source, target):
+        return pltpu.make_async_remote_copy(
+            src_ref=send_rows.at[layer, target],
+            dst_ref=recv_rows.at[layer, source],
+            send_sem=d_send.at[layer, offset],
+            recv_sem=d_recv.at[layer, offset],
+            device_id=(grp, target),
+            device_id_type=MESH,
+        )
+
+    def rows_own(layer):
+        return pltpu.make_async_copy(send_rows.at[layer, dev], recv_rows.at[layer, dev], d_own.at[layer])
+
+    for layer in range(layers):
+        for half in range(HALVES):
+            which = half * layers + layer
+            span = pl.ds(half * half_rows, half_rows)
+            wait_bytes(recv_back.at[layer, pl.ds(0, count - 1), :, span], c_recv.at[which])
+            wait_bytes(recv_back.at[layer, 0, :, span], c_own.at[which])
+
+        @pl.loop(0, RADIX)
+        def _(v0):
+            for part in range(2):
+                pieces = [
+                    recv_back[layer, k, part, pl.ds(v0, sub_rows, stride=RADIX), :] for k in range(count)
+                ]
+                hi, lo = high_low(jnp.concatenate(pieces, axis=0).T)
+                high[v0, :, part * depth : (part + 1) * depth] = hi
+                low[v0, :, part * depth : (part + 1) * depth] = lo
+
+        @pl.loop(0, tiles_y)
+        def _(n):
+            mid_y[n] = three_products(
+                high[:, :, : 2 * depth].reshape(RADIX * x_rows, 2 * depth),
+                low[:, :, : 2 * depth].reshape(RADIX * x_rows, 2 * depth),
+                table_iy[0, n],
+                table_iy[1, n],
+            ).reshape(RADIX, x_rows, width_y)
+
+        @pl.loop(0, x_rows // 8)
+        def _(chunk):
+            rows = pl.ds(pl.multiple_of(chunk * 8, 8), 8)
+            for lane in range(lane_blocks):
+                column = lane * LANES
+                lanes = slice(column, column + LANES)
+                within = slice(column % width_y, column % width_y + LANES)
+                tile = column // width_y
+                values = eight_point_to_real(
+                    [
+                        times(
+                            (mid_y[tile, v, rows, within], mid_y[tile + tiles_y // 2, v, rows, within]),
+                            (twiddle_iy[v, 0:1, lanes], twiddle_iy[v, 1:2, lanes]),
+                        )
+                        for v in range(RADIX)
+                    ]
+                )
+                for s in range(RADIX):
+                    send_rows[layer, s, rows, lanes] = values[s]
+
+        for offset in range(1, members):
+            rows_copy(layer, offset, dev, lax.rem(dev + offset, members)).start()
+        rows_own(layer).start()
+
+    def finish(layer, lane):
+        return pltpu.make_async_copy(
+            staged.at[lane], result_hbm.at[layer, :, pl.ds(lane * LANES, LANES)], done_sem.at[lane]
+        )
+
+    for layer in range(layers):
+        if layer > 0:
+            for lane in range(lane_blocks):
+                finish(layer - 1, lane).wait()
+        for offset in range(members):
+            source = lax.rem(dev + members - offset, members)
+            if offset == 0:
+                rows_own(layer).wait()
+            else:
+                rows_copy(layer, offset, source, lax.rem(dev + offset, members)).wait_recv()
+
+            @pl.loop(0, x_rows // 32)
+            def _(chunk):
+                for lane in range(lane_blocks):
+                    staged[lane, pl.ds(chunk * 32 * members + source, 32, stride=members), :] = recv_rows[
+                        layer, source, pl.ds(pl.multiple_of(chunk * 32, 32), 32), lane * LANES : (lane + 1) * LANES
+                    ]
+
+        for lane in range(lane_blocks):
+            finish(layer, lane).start()
+    for lane in range(lane_blocks):
+        finish(layers - 1, lane).wait()
+
+    for half in range(HALVES):
+        wait_bytes(send_spec.at[half, pl.ds(0, count - 1)], b_send.at[half])
+        for layer in range(layers):
+            wait_bytes(send_back.at[half, layer, pl.ds(0, count - 1)], c_send.at[half * layers + layer])
+    for layer in range(layers):
+        for offset in range(1, members):
+            rows_copy(layer, offset, dev, lax.rem(dev + offset, members)).wait_send()
+
+
+def tile_columns(table, width):
+    rows, columns = table.shape
+    return table.reshape(rows, columns // width, width).transpose(1, 0, 2)
+
+
+def fast_body(boundary_heat_flux, layer_kernel):
+    groups, members = lax.axis_size("grp"), lax.axis_size("dev")
+    count = groups * members
+    local_x, trail = boundary_heat_flux.shape
+    x_rows = local_x // members
+    layers, _, block_rows, width_x = layer_kernel.shape
+    width_y = trail * members
+    depth = block_rows * count // RADIX
+    points = width_x // RADIX
+    half_rows = block_rows // HALVES
+    bf16, f32 = jnp.bfloat16, jnp.float32
+    device_pos = lax.axis_index("grp") * members + lax.axis_index("dev")
+    first = jnp.logical_and(device_pos == 0, lax.broadcasted_iota(jnp.int32, (block_rows, LANES), 0) == 0)
+    weight = jnp.where(first, 1.0, 2.0).astype(f32) * (1.0 / (width_x * width_y))
+
+    forward = complex_table(trail, depth, trail, -1.0).T
+    forward = forward.reshape(2, count, HALVES, half_rows // RADIX, 2 * trail).transpose(2, 0, 1, 3, 4)
+    operands = (
+        boundary_heat_flux,
+        layer_kernel,
+        weight,
+        split_table(forward.reshape(HALVES, 2 * depth // HALVES, 2 * trail)),
+        split_table(tile_columns(complex_table(points, points, points, -1.0), 256)),
+        split_table(tile_columns(complex_table(points, points, points, 1.0), 256)),
+        split_table(tile_columns(complex_table(depth, trail, trail, 1.0), 256)),
+        twiddle_table(trail, width_y, -1.0),
+        twiddle_table(points, width_x, -1.0),
+        twiddle_table(trail, width_y, 1.0),
+    )
+    rows_shape = (layers, members, x_rows, trail)
+    buffers = [
+        ((trail // LANES, local_x, LANES), f32),
+        (rows_shape, f32),
+        (rows_shape, f32),
+        ((RADIX, x_rows, 2 * trail), bf16),
+        ((RADIX, x_rows, 2 * trail), bf16),
+        ((HALVES, count, 2, half_rows, x_rows), f32),
+        ((HALVES, count, 2, half_rows, x_rows), f32),
+        ((RADIX, half_rows, 2 * points), bf16),
+        ((RADIX, half_rows, 2 * points), bf16),
+        ((2 * points // 256, RADIX, half_rows, 256), f32),
+        ((layers, RADIX, half_rows, 2 * points), bf16),
+        ((layers, RADIX, half_rows, 2 * points), bf16),
+        ((HALVES, layers, count, 2, half_rows, x_rows), f32),
+        ((layers, count, 2, block_rows, x_rows), f32),
+        ((2 * trail // 256, RADIX, x_rows, 256), f32),
+    ] + [(a.shape, a.dtype) for a in operands[1:]]
+    dma = lambda *shape: pltpu.SemaphoreType.DMA(shape)
+    return pl.pallas_call(
+        functools.partial(whole_kernel, (groups, members)),
+        out_shape=jax.ShapeDtypeStruct((layers, local_x, trail), f32),
+        in_specs=[pl.BlockSpec(memory_space=pl.ANY)] * len(operands),
+        out_specs=pl.BlockSpec(memory_space=pl.ANY),
+        scratch_shapes=[pltpu.VMEM(shape, dtype) for shape, dtype in buffers]
+        + [
+            dma(len(operands) - 1),
+            dma(trail // LANES),
+            dma(PARTS_IN),
+            dma(PARTS_IN),
+            dma(HALVES),
+            dma(HALVES),
+            dma(HALVES),
+            dma(HALVES * layers),
+            dma(HALVES * layers),
+            dma(HALVES * layers),
+            dma(layers, members),
+            dma(layers, members),
+            dma(layers),
+            dma(trail // LANES),
+        ],
+        compiler_params=pltpu.CompilerParams(
+            collective_id=0, has_side_effects=True, vmem_limit_bytes=VMEM_LIMIT
+        ),
+    )(*operands)
+
+
 def solution(mesh):
     placed = (P("grp", "dev"), P(None, None, ("grp", "dev"), None))
+    groups, members = mesh.shape["grp"], mesh.shape["dev"]
+
+    def chosen(boundary_heat_flux, layer_kernel):
+        local_x, trail = boundary_heat_flux.shape
+        block_rows = layer_kernel.shape[2]
+        fits = (
+            members == RADIX
+            and local_x // members == LANES
+            and trail % LANES == 0
+            and groups * LANES * RADIX == layer_kernel.shape[3]
+            and block_rows % (16 * HALVES) == 0
+            and (groups * LANES) % 256 == 0
+            and trail % 256 == 0
+            and block_rows * groups % 32 == 0
+        )
+        return (fast_body if fits else body)(boundary_heat_flux, layer_kernel)
+
     return jax.shard_map(
-        body, mesh=mesh, in_specs=placed, out_specs=P(None, "grp", "dev"), check_vma=False
-    )
+        chosen, mesh=mesh, in_specs=placed, out_specs=P(None, "grp", "dev"), check_vma=False
+    )

time: 880 us -> 287 us (0.33)
  the two profiles are of different devices: /device:TPU:0 before, /device:TPU:9 now
where the time goes in v2:
time: 287 us
  Pallas kernels  282 us (98%)
  local copies, waits for them, and re-layouts  5.33 us (2%)
    pallas_call x1, Pallas kernels, fast_body(): pl.pallas_call(functools.partial(whole_kernel, (groups, members)), out_sh...  282 us

profile of v2, /device:TPU:9, one launch (start us, length us, event | category | flops | bytes accessed | tf_op | source)
XLA Modules:
  0.0 287.0 jit_solution(12564720685189426337)
XLA Ops:
  0.0 0.7 iota.7.weight_hbm
  0.7 281.6 %shard_map.91 = f32[2,1024,512]{2,1,0:T(8,128)} custom-call(f32[1024,512]{1,0:T(8,128)} %flux.1, f32[2,2,64,4096]{3,2,1,0:T(8,128)} %kernel_hbm.1, f32[64,128]{1,0:T(8,128)} %iota.7.weight_hbm, bf16[2,2,256,1024]{3,2,1,0:T(8,128)(2,1)} %constant.31.clone.fy_hbm, bf16[2,4,1024,256]{3,2,1,0:T(8,128)(2,1)} %constant.32.clone.in_hbm, ...), custom_call_target="tpu_custom_call" | custom-call | tf_op jit(solution)/shard_map/pallas_call | solution.py:735
  282.3 4.6 %copy.11 = f32[2,1024,512]{2,1,0:T(8,128)} copy(f32[2,1024,512]{2,1,0:T(8,128)} %shard_map.91) | data formatting | bytes 8388608
  (1 shorter events, 0.0 us)

commit v3 on v2

--- a/solution.py
+++ b/solution.py
@@ -480,6 +480,8 @@
                             at : at + quarter_rows, side * x_rows : (side + 1) * x_rows
                         ]
 
+        if half > 0:
+            wait_bytes(send_spec.at[half - 1, pl.ds(0, count - 1)], b_send.at[half - 1])
         send_all(
             send_spec.at[half], lambda k: recv_spec.at[half, k], b_send.at[half], b_recv.at[half], b_own.at[half]
         )
@@ -565,6 +567,8 @@
 
             which = half * layers + layer
             span = pl.ds(half * half_rows, half_rows)
+            if half == HALVES - 1 and layer > 0:
+                wait_bytes(send_back.at[half, layer - 1, pl.ds(0, count - 1)], c_send.at[which - 1])
             send_all(
                 send_back.at[half, layer],
                 lambda k: recv_back.at[layer, k, :, span],
@@ -671,9 +675,10 @@
         finish(layers - 1, lane).wait()
 
     for half in range(HALVES):
-        wait_bytes(send_spec.at[half, pl.ds(0, count - 1)], b_send.at[half])
         for layer in range(layers):
-            wait_bytes(send_back.at[half, layer, pl.ds(0, count - 1)], c_send.at[half * layers + layer])
+            if half < HALVES - 1 or layer == layers - 1:
+                wait_bytes(send_back.at[half, layer, pl.ds(0, count - 1)], c_send.at[half * layers + layer])
+    wait_bytes(send_spec.at[HALVES - 1, pl.ds(0, count - 1)], b_send.at[HALVES - 1])
     for layer in range(layers):
         for offset in range(1, members):
             rows_copy(layer, offset, dev, lax.rem(dev + offset, members)).wait_send()

time: 287 us -> 288 us (level)
  no operation moved by 1% of the time
where the time goes in v3:
time: 288 us; the launch traced here: 286 us
  Pallas kernels  281 us (98%)
  local copies, waits for them, and re-layouts  5.33 us (2%)
    pallas_call x1, Pallas kernels, fast_body(): pl.pallas_call(functools.partial(whole_kernel, (groups, members)), out_sh...  281 us

profile of v3, /device:TPU:9, one launch (start us, length us, event | category | flops | bytes accessed | tf_op | source)
XLA Modules:
  0.0 286.4 jit_solution(5558495529628698353)
XLA Ops:
  0.0 0.7 iota.7.weight_hbm
  0.7 281.1 %shard_map.91 = f32[2,1024,512]{2,1,0:T(8,128)} custom-call(f32[1024,512]{1,0:T(8,128)} %flux.1, f32[2,2,64,4096]{3,2,1,0:T(8,128)} %kernel_hbm.1, f32[64,128]{1,0:T(8,128)} %iota.7.weight_hbm, bf16[2,2,256,1024]{3,2,1,0:T(8,128)(2,1)} %constant.31.clone.fy_hbm, bf16[2,4,1024,256]{3,2,1,0:T(8,128)(2,1)} %constant.32.clone.in_hbm, ...), custom_call_target="tpu_custom_call" | custom-call | tf_op jit(solution)/shard_map/pallas_call | solution.py:740
  281.8 4.6 %copy.11 = f32[2,1024,512]{2,1,0:T(8,128)} copy(f32[2,1024,512]{2,1,0:T(8,128)} %shard_map.91) | data formatting | bytes 8388608
  (1 shorter events, 0.0 us)

commit v4 on v2

--- a/solution.py
+++ b/solution.py
@@ -328,7 +328,7 @@
     return dot(high, table_high) + dot(high, table_low) + dot(low, table_high)
 
 
-PARTS_IN = 4
+PARTS_IN = 8
 HALVES = 2
 
 

time: 287 us -> 289 us (level)
  no operation moved by 1% of the time
where the time goes in v4:
time: 289 us
  Pallas kernels  283 us (98%)
  local copies, waits for them, and re-layouts  5.33 us (2%)
    pallas_call x1, Pallas kernels, fast_body(): pl.pallas_call(functools.partial(whole_kernel, (groups, members)), out_sh...  283 us

profile of v4, /device:TPU:9, one launch (start us, length us, event | category | flops | bytes accessed | tf_op | source)
XLA Modules:
  0.0 288.7 jit_solution(17890306372197093781)
XLA Ops:
  0.0 0.7 iota.7.weight_hbm
  0.7 283.3 %shard_map.91 = f32[2,1024,512]{2,1,0:T(8,128)} custom-call(f32[1024,512]{1,0:T(8,128)} %flux.1, f32[2,2,64,4096]{3,2,1,0:T(8,128)} %kernel_hbm.1, f32[64,128]{1,0:T(8,128)} %iota.7.weight_hbm, bf16[2,2,256,1024]{3,2,1,0:T(8,128)(2,1)} %constant.31.clone.fy_hbm, bf16[2,4,1024,256]{3,2,1,0:T(8,128)(2,1)} %constant.32.clone.in_hbm, ...), custom_call_target="tpu_custom_call" | custom-call | tf_op jit(solution)/shard_map/pallas_call | solution.py:735
  284.0 4.6 %copy.11 = f32[2,1024,512]{2,1,0:T(8,128)} copy(f32[2,1024,512]{2,1,0:T(8,128)} %shard_map.91) | data formatting | bytes 8388608
  (1 shorter events, 0.0 us)
